TPU v7x, 256 devices: a whole 4x4x8 slice. The times are simulated.
256 devices in a mesh: dp: 32 (over x, y, core), vocab: 8 (over z).
Axes of the slice: x: 4, y: 4, z: 8, core: 2. Of those that a mesh axis runs over, the one named last changes fastest.
Arguments:
- student_hidden: bfloat16 [768, 3584], P('dp'), may hold values from -110 to 110
- teacher_hidden: bfloat16 [768, 4608], P('dp'), may hold values from -110 to 110
- student_head: bfloat16 [3584, 131072], P(None, ('dp', 'vocab')), may hold values from -0.09375 to 0.09375
- teacher_head: bfloat16 [4608, 131072], P(None, ('dp', 'vocab')), may hold values from -0.09375 to 0.09375
- live_count: int32 [32], P('dp'), may hold values from 1 to 24, as said below
- teacher_count: int32 [32], P('dp'), may hold values from 1 to 24, as said below
- teacher_dest: int32 [768], P('dp'), may hold values from 0 to 767, as said below
Outputs:
- distill_loss: float32 [], replicated
- grad_hidden: bfloat16 [768, 3584], P('dp', 'vocab')
- grad_head: bfloat16 [3584, 131072], P(None, ('dp', 'vocab'))
Inputs may be any that keep to these rules, and one draw needn't show every extreme that they name: Shard s's covered tokens are its first live_count[s] tokens; the counts sum to 384. Data shard j's filled teacher row slots are its first teacher_count[j] slots; the counts sum to 384. `teacher_dest`: A filled slot names the global index of a covered token; every covered token is named by exactly one filled slot. Unfilled slots hold arbitrary indices.
All inputs are finite; a program needn't handle non-finite values.
Results may differ from a plain program's by a relative error of at most 0.014.
Values may be sent and summed in bfloat16 or wider, within the bound.
No kernel may reach another device: no remote copies, remote signals or barrier semaphores. Data moves between devices by JAX's collectives and lax.ppermute only.
A program may use at most 128 MiB of HBM per device.

v0:
```python
import jax
import jax.numpy as jnp
from jax import lax
from jax.sharding import PartitionSpec as P

loss_scale = 65536.0


def per_device(
    student_hidden,
    teacher_hidden,
    student_head,
    teacher_head,
    live_count,
    teacher_count,
    teacher_dest,
):
    tok_dev = student_hidden.shape[0]
    data_size = lax.axis_size("dp")
    token_count = tok_dev * data_size
    live_total = token_count // 2
    grad_scale = loss_scale / live_total
    live_all, teach_all, dest_all = (
        lax.all_gather(live_count, "dp", axis=0, tiled=True),
        lax.all_gather(teacher_count, "dp", axis=0, tiled=True),
        lax.all_gather(teacher_dest, "dp", axis=0, tiled=True),
    )
    position = lax.broadcasted_iota(jnp.int32, (data_size, tok_dev), 1)
    live_flag = (position < live_all[:, None]).reshape(-1)
    slot_ok = (position < teach_all[:, None]).reshape(-1)
    gathered = lax.all_gather(student_hidden, "dp", axis=0, tiled=True)
    vocab_rows = student_head.shape[1]
    student_logits = jnp.dot(gathered, student_head, preferred_element_type=jnp.float32)
    packed = jnp.dot(
        lax.all_gather(teacher_hidden, "dp", axis=0, tiled=True),
        teacher_head,
        preferred_element_type=jnp.float32,
    )
    target = jnp.where(slot_ok, dest_all, token_count)
    teacher_logits = (
        jnp.zeros((token_count, vocab_rows), jnp.float32).at[target].set(packed, mode="drop")
    )
    teacher_top, student_top = lax.pmax(
        (jnp.max(teacher_logits, axis=1), jnp.max(student_logits, axis=1)), ("dp", "vocab")
    )
    teacher_weights = jnp.exp(teacher_logits - teacher_top[:, None])
    teacher_sum, student_sum, cross_sum = lax.psum(
        (
            jnp.sum(teacher_weights, axis=1),
            jnp.sum(jnp.exp(student_logits - student_top[:, None]), axis=1),
            jnp.sum(teacher_weights * (teacher_logits - student_logits), axis=1),
        ),
        ("dp", "vocab"),
    )
    teacher_norm = teacher_top + jnp.log(teacher_sum)
    student_norm = student_top + jnp.log(student_sum)
    divergence = cross_sum / teacher_sum - teacher_norm + student_norm
    distill_loss = jnp.sum(jnp.where(live_flag, divergence, 0.0)) / live_total
    probs_gap = jnp.exp(student_logits - student_norm[:, None]) - jnp.exp(
        teacher_logits - teacher_norm[:, None]
    )
    logit_grad = jnp.where(live_flag[:, None], probs_gap * grad_scale, 0.0).astype(jnp.bfloat16)
    grad_head = lax.dot_general(
        gathered, logit_grad, (((0,), (0,)), ((), ())), preferred_element_type=jnp.float32
    ).astype(jnp.bfloat16)
    columns = student_head.shape[0] // lax.axis_size("vocab")
    summed = lax.psum(
        lax.dot_general(
            logit_grad, student_head, (((1,), (1,)), ((), ())), preferred_element_type=jnp.float32
        ),
        ("dp", "vocab"),
    )
    own_block = lax.dynamic_slice(
        summed,
        (lax.axis_index("dp") * tok_dev, lax.axis_index("vocab") * columns),
        (tok_dev, columns),
    )
    return (distill_loss, own_block.astype(jnp.bfloat16), grad_head)


def solution(mesh):
    return jax.shard_map(
        per_device,
        mesh=mesh,
        in_specs=(
            P("dp", None),
            P("dp", None),
            P(None, ("dp", "vocab")),
            P(None, ("dp", "vocab")),
            P("dp"),
            P("dp"),
            P("dp"),
        ),
        out_specs=(P(), P("dp", "vocab"), P(None, ("dp", "vocab"))),
        check_vma=False,
    )
```

profile of v0, /device:TPU:1, one launch (start us, length us, event | category | flops | bytes accessed | tf_op | source)
XLA Modules:
  0.0 473.6 jit_solution(16044244641711408158)
XLA Ops:
  7.2 0.0 all-gather.5.cloned.1.call-start
  7.2 0.7 all-gather.5.cloned.1.call-update
  7.9 0.0 all-gather.3.cloned.1.call-start
  7.9 0.7 all-gather.3.cloned.1.call-update
  9.9 1.3 dynamic-slice
  11.9 0.8 dynamic-update-slice
  12.6 0.8 dynamic-update-slice.1
  13.4 0.8 dynamic-update-slice.2
  14.2 14.7 %all-reduce.3 = (s32[32]{0:T(128)S(1)}, s32[32]{0:T(128)S(1)}, s32[768]{0:T(1024)S(1)}) all-reduce(s32[32]{0:T(128)S(1)} %dynamic-update-slice, s32[32]{0:T(128)S(1)} %dynamic-update-slice.1, s32[768]{0:T(1024)S(1)} %dynamic-update-slice.2), channel_id=1, replica_groups=mesh['dp'=32,'vocab'=8] {'dp'}, use_global_device_ids=true, to_apply=%add | all-reduce | flops 832 | bytes 6656
  28.9 0.1 iota_compare_fusion.1
  29.0 0.1 lt.42
  29.1 0.1 iota_compare_fusion
  29.2 0.1 lt.45
  29.3 38.4 %all-gather.5.cloned.1.call-done = bf16[768,3584]{1,0:T(8,128)(2,1)} async-done(((bf16[24,3584]{1,0:T(8,128)(2,1)}), bf16[768,3584]{1,0:T(8,128)(2,1)}) %all-gather.5.cloned.1.call-update) | async-done | bytes 5505040 | tf_op jit(solution)/shard_map/all_gather | solution.py:31
  67.7 7.9 %fusion.4 = (f32[768]{0:T(1024)S(1)}, f32[768,512]{0,1:T(8,128)}) fusion(bf16[768,3584]{1,0:T(8,128)(2,1)} %all-gather.5.cloned.1.call-done, bf16[3584,512]{1,0:T(8,128)(2,1)} %param.9), kind=kOutput, calls=%fused_computation.17 | convolution fusion | flops 2818964736 | bytes 10750976 | tf_op jit(solution)/shard_map/dot_general | solution.py:33
  75.6 49.5 %all-gather.3.cloned.1.call-done = bf16[768,4608]{1,0:T(8,128)(2,1)} async-done(((bf16[24,4608]{1,0:T(8,128)(2,1)}), bf16[768,4608]{1,0:T(8,128)(2,1)}) %all-gather.3.cloned.1.call-update) | async-done | bytes 7077904 | tf_op jit(solution)/shard_map/all_gather | solution.py:35
  125.1 9.3 %fusion.5 = f32[768,512]{1,0:T(8,128)} fusion(bf16[768,4608]{1,0:T(8,128)(2,1)} %all-gather.3.cloned.1.call-done, bf16[4608,512]{1,0:T(8,128)(2,1)} %param.10), kind=kOutput, calls=%fused_computation.18 | convolution fusion | flops 3623878656 | bytes 13369344 | tf_op jit(solution)/shard_map/dot_general | solution.py:34
  134.4 6.6 %scatter_custom_fusion = f32[768,512]{1,0:T(8,128)S(1)} fusion(s32[768]{0:T(1024)S(1)} %compare_select_fusion, f32[768,512]{1,0:T(8,128)} %fusion.5, f32[]{:T(128)} %constant.12.clone.1), kind=kCustom, calls=%fused_computation.8 | custom fusion | bytes 1573376 | tf_op jit(solution)/shard_map/scatter | solution.py:41
  141.0 0.5 copy.12
  141.5 0.2 reduce_max.18
  141.6 75.6 %all-reduce.6 = (f32[768]{0:T(1024)S(1)}, f32[768]{0:T(1024)S(1)}) all-reduce(f32[768]{0:T(1024)S(1)} %get-tuple-element.21, f32[768]{0:T(1024)S(1)} %reduce_max.18), channel_id=1, replica_groups=mesh['dp'=32,'vocab'=8] {'dp','vocab'}, use_global_device_ids=true, to_apply=%region_8.9 | all-reduce | flops 1536 | bytes 12288 | tf_op jit(solution)/shard_map/pmax | solution.py:43
  217.3 0.0 copy-start
  217.3 2.1 multiply_reduce_fusion
  219.4 74.5 %all-reduce.5 = (f32[768]{0:T(1024)S(1)}, f32[768]{0:T(1024)S(1)}) all-reduce(f32[768]{0:T(1024)S(1)} %get-tuple-element.11, f32[768]{0:T(1024)S(1)} %get-tuple-element.10), channel_id=1, replica_groups=mesh['dp'=32,'vocab'=8] {'dp','vocab'}, use_global_device_ids=true, to_apply=%region_10.11 | all-reduce | flops 1536 | bytes 12288 | tf_op jit(solution)/shard_map/psum | solution.py:47
  293.9 0.0 copy-done
  293.9 0.0 slice-start
  293.9 0.5 select_convert_fusion
  294.4 0.0 slice-start.1
  294.4 8.2 %fusion.6 = f32[768,3584]{1,0:T(8,128)} fusion(bf16[768,512]{0,1:T(8,128)(2,1)S(1)} %select_convert_fusion, bf16[3584,512]{1,0:T(8,128)(2,1)} %param.9), kind=kOutput, calls=%fused_computation.19 | convolution fusion | flops 2818572288 | bytes 15466496 | tf_op jit(solution)/shard_map/dot_general | solution.py:68
  302.6 0.0 slice-done
  302.6 0.0 slice-done.1
  302.6 4.5 fusion
  307.1 5.9 %copy.15 = bf16[3584,512]{1,0:T(8,128)(2,1)} copy(bf16[3584,512]{0,1:T(8,128)(2,1)} %fusion) | data formatting | bytes 7340032
  313.0 149.9 %all-reduce.8 = (f32[768]{0:T(1024)S(1)}, bf16[768,3584]{1,0:T(8,128)(2,1)}) all-reduce(f32[768]{0:T(1024)S(1)} %get-tuple-element.9, f32[768,3584]{1,0:T(8,128)} %fusion.6), channel_id=1, replica_groups=mesh['dp'=32,'vocab'=8] {'dp','vocab'}, use_global_device_ids=true, to_apply=%region_4.5 | all-reduce | flops 2753280 | bytes 16521216 | tf_op jit(solution)/shard_map/psum | solution.py:47
  462.9 0.6 select_reduce_fusion
  464.2 1.5 dynamic_slice.5
  (6 shorter events, 0.0 us)
Async XLA Ops:
  7.2 60.5 %all-gather.5.cloned.1.call-start = ((), (), s32[]{:S(2)}) async-start(), calls=%async_computation.1 | async-start | bytes 5677056 | tf_op jit(solution)/shard_map/all_gather | solution.py:31
  7.9 117.2 %all-gather.3.cloned.1.call-start = ((), (), s32[]{:S(2)}) async-start(), calls=%async_computation | async-start | bytes 7299072 | tf_op jit(solution)/shard_map/all_gather | solution.py:35
  217.3 76.6 %copy-start = (f32[768,512]{0,1:T(8,128)S(1)}, f32[768,512]{0,1:T(8,128)}, u32[]{:S(2)}) copy-start(f32[768,512]{0,1:T(8,128)} %get-tuple-element.22) | copy-start | bytes 4718596
  293.9 8.7 %slice-start = ((s8[5505024]{0:T(1024)(128)(4,1)}), s8[4194304]{0:T(1024)(128)(4,1)S(1)}, s32[]{:S(2)}) async-start(s8[5505024]{0:T(1024)(128)(4,1)} %bitcast.13), calls=%async_computation.2 | async-start | bytes 8388608
  294.4 8.2 %slice-start.1 = ((s8[5505024]{0:T(1024)(128)(4,1)}), s8[1310720]{0:T(1024)(128)(4,1)S(1)}, s32[]{:S(2)}) async-start(s8[5505024]{0:T(1024)(128)(4,1)} %bitcast.13), calls=%async_computation.3 | async-start | bytes 2621440
Sparse Core Ops, SparseCore 0:
  10.5 57.1 all-gather.4
  70.2 54.7 all-gather.2
where the time goes:
time: 474 us
  blocking collectives  315 us (66%)
  waiting for transfers between devices  89.3 us (19%)
  matrix products  29.9 us (6%)
  local copies, waits for them, and re-layouts  18.2 us (4%)
  between operations  17.9 us (4%)
    psum x2, blocking collectives, per_device(): lax.psum((jnp.sum(teacher_weights, axis=1), jnp.sum(jnp.exp(student_logit...  224 us
    pmax x1, blocking collectives, per_device(): lax.pmax((jnp.max(teacher_logits, axis=1), jnp.max(student_logits, axis=1...  75.6 us
    all_gather x1, waiting for transfers between devices, per_device(): lax.all_gather(teacher_hidden, 'dp', axis=0, tiled=True)  49.5 us
    all_gather x1, waiting for transfers between devices, per_device(): gathered = lax.all_gather(student_hidden, 'dp', axis=0, tiled=True)  38.4 us
    unnamed x1, blocking collectives  14.7 us
    unnamed x14, local copies, waits for them, and re-layouts  9.54 us
  transfers between devices with their start and end apart: 2, of which 2 were waited for; matrix products, arithmetic and copies ran while one was open for 2% of the time, Pallas kernels for 0%

commit v1 on v0

--- a/solution.py
+++ b/solution.py
@@ -44,13 +44,17 @@
         (jnp.max(teacher_logits, axis=1), jnp.max(student_logits, axis=1)), ("dp", "vocab")
     )
     teacher_weights = jnp.exp(teacher_logits - teacher_top[:, None])
-    teacher_sum, student_sum, cross_sum = lax.psum(
+
+    def numbers_get(matrix):
+        out_arr = lax.psum(lax.psum(matrix, "vocab"), axis_name="dp")
+        return out_arr
+
+    teacher_sum, student_sum, cross_sum = numbers_get(
         (
             jnp.sum(teacher_weights, axis=1),
             jnp.sum(jnp.exp(student_logits - student_top[:, None]), axis=1),
             jnp.sum(teacher_weights * (teacher_logits - student_logits), axis=1),
-        ),
-        ("dp", "vocab"),
+        )
     )
     teacher_norm = teacher_top + jnp.log(teacher_sum)
     student_norm = student_top + jnp.log(student_sum)

time: 474 us -> 547 us (1.15)
  blocking collectives: 315 us -> 389 us
    psum x2 -> x3, blocking collectives: 224 us -> 299 us  [the longest x1 151 us: per_device(): lax.psum(lax.dot_general(logit_grad, student_head, (((1,), (1,)), ((), ()...]
where the time goes in v1:
time: 547 us
  blocking collectives  389 us (71%)
  waiting for transfers between devices  89.3 us (16%)
  matrix products  27.5 us (5%)
  local copies, waits for them, and re-layouts  19.2 us (4%)
  between operations  17.8 us (3%)
    psum x1, blocking collectives, per_device(): lax.psum(lax.dot_general(logit_grad, student_head, (((1,), (1,)), ((), ()...  151 us
    psum x2, blocking collectives, numbers_get(): out_arr = lax.psum(lax.psum(matrix, 'vocab'), axis_name='dp')  148 us
    pmax x1, blocking collectives, per_device(): lax.pmax((jnp.max(teacher_logits, axis=1), jnp.max(student_logits, axis=1...  75.6 us
    all_gather x1, waiting for transfers between devices, per_device(): lax.all_gather(teacher_hidden, 'dp', axis=0, tiled=True)  49.5 us
    all_gather x1, waiting for transfers between devices, per_device(): gathered = lax.all_gather(student_hidden, 'dp', axis=0, tiled=True)  38.4 us
    unnamed x1, blocking collectives  14.7 us
  transfers between devices with their start and end apart: 2, of which 2 were waited for; matrix products, arithmetic and copies ran while one was open for 2% of the time, Pallas kernels for 0%

profile of v1, /device:TPU:1, one launch (start us, length us, event | category | flops | bytes accessed | tf_op | source)
XLA Modules:
  0.0 546.6 jit_solution(4546018690809414506)
XLA Ops:
  7.2 0.0 all-gather.5.cloned.1.call-start
  7.2 0.7 all-gather.5.cloned.1.call-update
  7.9 0.0 all-gather.3.cloned.1.call-start
  7.9 0.7 all-gather.3.cloned.1.call-update
  9.9 1.3 dynamic-slice
  11.9 0.8 dynamic-update-slice
  12.6 0.8 dynamic-update-slice.1
  13.4 0.8 dynamic-update-slice.2
  14.2 14.7 %all-reduce.3 = (s32[32]{0:T(128)S(1)}, s32[32]{0:T(128)S(1)}, s32[768]{0:T(1024)S(1)}) all-reduce(s32[32]{0:T(128)S(1)} %dynamic-update-slice, s32[32]{0:T(128)S(1)} %dynamic-update-slice.1, s32[768]{0:T(1024)S(1)} %dynamic-update-slice.2), channel_id=1, replica_groups=mesh['dp'=32,'vocab'=8] {'dp'}, use_global_device_ids=true, to_apply=%add | all-reduce | flops 832 | bytes 6656
  28.9 0.1 iota_compare_fusion.1
  29.0 0.1 lt.42
  29.1 0.1 iota_compare_fusion
  29.2 0.1 lt.45
  29.3 38.4 %all-gather.5.cloned.1.call-done = bf16[768,3584]{1,0:T(8,128)(2,1)} async-done(((bf16[24,3584]{1,0:T(8,128)(2,1)}), bf16[768,3584]{1,0:T(8,128)(2,1)}) %all-gather.5.cloned.1.call-update) | async-done | bytes 5505040 | tf_op jit(solution)/shard_map/all_gather | solution.py:31
  67.7 7.9 %fusion.4 = (f32[768]{0:T(1024)S(1)}, f32[768,512]{0,1:T(8,128)}) fusion(bf16[768,3584]{1,0:T(8,128)(2,1)} %all-gather.5.cloned.1.call-done, bf16[3584,512]{1,0:T(8,128)(2,1)} %param.9), kind=kOutput, calls=%fused_computation.17 | convolution fusion | flops 2818964736 | bytes 10750976 | tf_op jit(solution)/shard_map/dot_general | solution.py:33
  75.6 49.5 %all-gather.3.cloned.1.call-done = bf16[768,4608]{1,0:T(8,128)(2,1)} async-done(((bf16[24,4608]{1,0:T(8,128)(2,1)}), bf16[768,4608]{1,0:T(8,128)(2,1)}) %all-gather.3.cloned.1.call-update) | async-done | bytes 7077904 | tf_op jit(solution)/shard_map/all_gather | solution.py:35
  125.1 9.3 %fusion.5 = f32[768,512]{1,0:T(8,128)} fusion(bf16[768,4608]{1,0:T(8,128)(2,1)} %all-gather.3.cloned.1.call-done, bf16[4608,512]{1,0:T(8,128)(2,1)} %param.10), kind=kOutput, calls=%fused_computation.18 | convolution fusion | flops 3623878656 | bytes 13369344 | tf_op jit(solution)/shard_map/dot_general | solution.py:34
  134.4 6.6 %scatter_custom_fusion = f32[768,512]{1,0:T(8,128)S(1)} fusion(s32[768]{0:T(1024)S(1)} %compare_select_fusion, f32[768,512]{1,0:T(8,128)} %fusion.5, f32[]{:T(128)} %constant.12.clone.1), kind=kCustom, calls=%fused_computation.8 | custom fusion | bytes 1573376 | tf_op jit(solution)/shard_map/scatter | solution.py:41
  140.9 0.5 copy.12
  141.4 0.2 reduce_max.18
  141.6 75.6 %all-reduce.4 = (f32[768]{0:T(1024)S(1)}, f32[768]{0:T(1024)S(1)}) all-reduce(f32[768]{0:T(1024)S(1)} %get-tuple-element.26, f32[768]{0:T(1024)S(1)} %reduce_max.18), channel_id=1, replica_groups=mesh['dp'=32,'vocab'=8] {'dp','vocab'}, use_global_device_ids=true, to_apply=%region_10.11 | all-reduce | flops 1536 | bytes 12288 | tf_op jit(solution)/shard_map/pmax | solution.py:43
  217.2 0.0 copy-start
  217.2 2.1 multiply_reduce_fusion
  219.3 22.0 %all-reduce.6 = (f32[768]{0:T(1024)S(1)}, f32[768]{0:T(1024)S(1)}, f32[768]{0:T(1024)S(1)}) all-reduce(f32[768]{0:T(1024)S(1)} %get-tuple-element.11, f32[768]{0:T(1024)S(1)} %get-tuple-element.10, f32[768]{0:T(1024)S(1)} %get-tuple-element.9), channel_id=1, replica_groups=mesh['dp'=32,'vocab'=8] {'vocab'}, use_global_device_ids=true, to_apply=%region_12.13 | all-reduce | flops 2304 | bytes 18432 | tf_op jit(solution)/shard_map/psum | solution.py:49
  241.3 126.0 %all-reduce.5 = (f32[768]{0:T(1024)S(1)}, f32[768]{0:T(1024)S(1)}, f32[768]{0:T(1024)S(1)}) all-reduce(f32[768]{0:T(1024)S(1)} %get-tuple-element.20, f32[768]{0:T(1024)S(1)} %get-tuple-element.21, f32[768]{0:T(1024)S(1)} %get-tuple-element.22), channel_id=1, replica_groups=mesh['dp'=32,'vocab'=8] {'dp'}, use_global_device_ids=true, to_apply=%region_13.14 | all-reduce | flops 2304 | bytes 18432 | tf_op jit(solution)/shard_map/psum | solution.py:49
  367.3 0.0 copy-start.1
  367.3 0.6 select_reduce_fusion
  367.9 0.0 copy-done
  367.9 0.0 slice-start
  367.9 0.5 select_convert_fusion
  368.4 0.9 copy-done.1
  369.4 0.0 slice-start.1
  369.4 5.8 %fusion.6 = f32[768,3584]{1,0:T(8,128)} fusion(bf16[768,512]{0,1:T(8,128)(2,1)S(1)} %select_convert_fusion, bf16[3584,512]{1,0:T(8,128)(2,1)S(1)} %copy-done.1), kind=kOutput, calls=%fused_computation.19 | convolution fusion | flops 2818572288 | bytes 15466496 | tf_op jit(solution)/shard_map/dot_general | solution.py:72
  375.1 0.0 slice-done
  375.1 0.0 slice-done.1
  375.1 4.5 fusion
  379.6 5.9 %copy.15 = bf16[3584,512]{1,0:T(8,128)(2,1)} copy(bf16[3584,512]{0,1:T(8,128)(2,1)} %fusion) | data formatting | bytes 7340032
  385.6 151.0 %all-reduce.8 = bf16[768,3584]{1,0:T(8,128)(2,1)} all-reduce(f32[768,3584]{1,0:T(8,128)} %fusion.6), channel_id=1, replica_groups=mesh['dp'=32,'vocab'=8] {'dp','vocab'}, use_global_device_ids=true, to_apply=%region_15.16 | all-reduce | flops 2752512 | bytes 16515072 | tf_op jit(solution)/shard_map/psum | solution.py:71
  537.2 1.5 dynamic_slice.5
  (5 shorter events, 0.0 us)
Async XLA Ops:
  7.2 60.5 %all-gather.5.cloned.1.call-start = ((), (), s32[]{:S(2)}) async-start(), calls=%async_computation.1 | async-start | bytes 5677056 | tf_op jit(solution)/shard_map/all_gather | solution.py:31
  7.9 117.2 %all-gather.3.cloned.1.call-start = ((), (), s32[]{:S(2)}) async-start(), calls=%async_computation | async-start | bytes 7299072 | tf_op jit(solution)/shard_map/all_gather | solution.py:35
  217.2 150.7 %copy-start = (f32[768,512]{0,1:T(8,128)S(1)}, f32[768,512]{0,1:T(8,128)}, u32[]{:S(2)}) copy-start(f32[768,512]{0,1:T(8,128)} %get-tuple-element.27) | copy-start | bytes 4718596
  367.3 2.0 copy-start.1
  367.9 7.2 %slice-start = ((s8[5505024]{0:T(1024)(128)(4,1)}), s8[4194304]{0:T(1024)(128)(4,1)S(1)}, s32[]{:S(2)}) async-start(s8[5505024]{0:T(1024)(128)(4,1)} %bitcast.13), calls=%async_computation.2 | async-start | bytes 8388608
  369.4 5.8 %slice-start.1 = ((s8[5505024]{0:T(1024)(128)(4,1)}), s8[1310720]{0:T(1024)(128)(4,1)S(1)}, s32[]{:S(2)}) async-start(s8[5505024]{0:T(1024)(128)(4,1)} %bitcast.13), calls=%async_computation.3 | async-start | bytes 2621440
Sparse Core Ops, SparseCore 0:
  10.5 57.1 all-gather.4
  70.2 54.7 all-gather.2
